TPU v7x, 32 devices: a whole 2x2x4 slice. The times are simulated.
32 devices in a mesh: tm: 8 (over y, x, core), space: 4 (over z).
Axes of the slice: x: 2, y: 2, z: 4, core: 2. Of those that a mesh axis runs over, the one named last changes fastest.
Arguments:
- queries: bfloat16 [8, 1024, 512], P('tm', 'space'), may hold values from -8 to 8
- key_tokens: bfloat16 [8, 1024, 512], P('tm', 'space'), may hold values from -8 to 8
- values: bfloat16 [8, 1024, 512], P('tm', 'space'), may hold values from -8 to 8
- near_list: int32 [8, 4, 8], replicated, may hold values from 0 to 11, as said below
- near_count: int32 [8, 4], replicated, may hold values from 1 to 8, as said below
- dist_band: int32 [8], replicated, may hold values from 0 to 3, as said below
- band_factor: int32 [3], replicated, may hold values from 1 to 4, as said below
Outputs:
- attended: bfloat16 [8, 1024, 512], P('tm', 'space')
Inputs may be any that keep to these rules, and one draw needn't show every extreme that they name: `near_list`: each entry is distinct within its list, never names a frame outside 0 to 7, and the first entry of block b is block b of the same frame. `near_count`: some query block of some frame lists 8 live blocks. `dist_band`: nondecreasing in the distance; 0 exactly for distances 0 and 1, 3 at distance 8 - 1. `band_factor`: each entry is 1, 2 or 4, and some entry is 4.
All inputs are finite; a program needn't handle non-finite values.
Results may differ from a plain program's by a relative error of at most 0.0028.
The roundings to bfloat16 on the way count: a program that leaves them out, or rounds other values in their place, can miss the bound.
Values may be sent and summed in bfloat16 or wider, within the bound.
A program may use at most 64 MiB of HBM per device.

v0:
```python
import math

import jax
import jax.numpy as jnp
from jax import lax
from jax.sharding import PartitionSpec as P

HD = 128
POOL = 128


lowest_score = -1e30


def extended(block, sides, width):
    for axis, dim in sides:
        count = lax.axis_size(axis)
        forward = [(i, i + 1) for i in range(count - 1)]
        backward = [(target, source) for source, target in forward]
        low = lax.ppermute(
            lax.slice_in_dim(block, block.shape[dim] - width, None, axis=dim), axis, forward
        )
        high = lax.ppermute(lax.slice_in_dim(block, 0, width, axis=dim), axis, backward)
        block = jnp.concatenate([low, block, high], axis=dim)
    return block


def lookup(table_values, positions):
    slot_ids = jnp.arange(table_values.shape[0], dtype=jnp.int32)
    picked = jnp.where(positions[:, None] == slot_ids[None, :], table_values[None, :], 0)
    return jnp.sum(picked, axis=1)


def coarsen(pooled, factor):
    frame_count, far_rows, head_count, head_size = pooled.shape
    widened = pooled.astype(jnp.float32)
    pair_means = jnp.mean(
        widened.reshape(frame_count, far_rows // 2, 2, head_count, head_size), axis=2
    ).astype(jnp.bfloat16)
    quad_means = jnp.mean(
        widened.reshape(frame_count, far_rows // 4, 4, head_count, head_size), axis=2
    ).astype(jnp.bfloat16)
    pair_means = jnp.repeat(pair_means, 2, axis=1)
    quad_means = jnp.repeat(quad_means, 4, axis=1)
    choose_factor = factor[:, None, None, None]
    return jnp.where(
        choose_factor == 1, pooled, jnp.where(choose_factor == 2, pair_means, quad_means)
    )


def attend_block(query_rows, near_k, near_v, near_ok, far_k, far_v, far_bias, far_ok):
    score_scale = 1.0 / math.sqrt(query_rows.shape[-1])
    near_scores = (
        jnp.einsum("bhd,khd->hbk", query_rows, near_k, preferred_element_type=jnp.float32)
        * score_scale
    )
    far_scores = (
        jnp.einsum("bhd,khd->hbk", query_rows, far_k, preferred_element_type=jnp.float32)
        * score_scale
        + far_bias[None, None, :]
    )
    near_scores = jnp.where(near_ok[None, None, :], near_scores, lowest_score)
    far_scores = jnp.where(far_ok[None, None, :], far_scores, lowest_score)
    row_top = jnp.maximum(
        jnp.max(near_scores, axis=-1, keepdims=True), jnp.max(far_scores, axis=-1, keepdims=True)
    )
    near_weights = jnp.where(near_ok[None, None, :], jnp.exp(near_scores - row_top), 0.0)
    far_weights = jnp.where(far_ok[None, None, :], jnp.exp(far_scores - row_top), 0.0)
    denominator = jnp.sum(near_weights, axis=-1) + jnp.sum(far_weights, axis=-1)
    weighted = jnp.einsum(
        "hbk,khd->bhd",
        near_weights.astype(jnp.bfloat16),
        near_v,
        preferred_element_type=jnp.float32,
    )
    weighted = weighted + jnp.einsum(
        "hbk,khd->bhd", far_weights.astype(jnp.bfloat16), far_v, preferred_element_type=jnp.float32
    )
    return (weighted / jnp.transpose(denominator)[:, :, None]).astype(jnp.bfloat16)


def attend_frame(
    query_frame,
    key_rim,
    value_rim,
    pooled_k,
    pooled_v,
    lists,
    counts,
    dist_band,
    band_factor,
    frame_index,
):
    frame_tokens, head_count, head_size = query_frame.shape
    block_count, list_length = lists.shape
    block_rows = frame_tokens // block_count
    frame_count, far_rows = (pooled_k.shape[0], pooled_k.shape[1])
    distance = jnp.abs(jnp.arange(frame_count, dtype=jnp.int32) - frame_index)
    band_index = lookup(dist_band, distance)
    factor = jnp.maximum(lookup(band_factor, band_index - 1), 1)
    far_k = coarsen(pooled_k, factor).reshape(frame_count * far_rows, head_count, head_size)
    far_v = coarsen(pooled_v, factor).reshape(frame_count * far_rows, head_count, head_size)
    far_bias = jnp.repeat(-jnp.log(factor.astype(jnp.float32)), far_rows)
    far_ok = jnp.repeat(distance >= 2, far_rows)
    key_blocks = key_rim.reshape(3 * block_count, block_rows, head_count, head_size)
    value_blocks = value_rim.reshape(3 * block_count, block_rows, head_count, head_size)

    def one_block(block_index):
        block_ids = lax.dynamic_index_in_dim(lists, block_index, 0, keepdims=False)
        live_slots = lax.dynamic_index_in_dim(counts, block_index, 0, keepdims=False)
        near_k = jnp.take(key_blocks, block_ids, axis=0).reshape(
            list_length * block_rows, head_count, head_size
        )
        near_v = jnp.take(value_blocks, block_ids, axis=0).reshape(
            list_length * block_rows, head_count, head_size
        )
        near_ok = jnp.repeat(jnp.arange(list_length, dtype=jnp.int32) < live_slots, block_rows)
        query_rows = lax.dynamic_slice_in_dim(query_frame, block_index * block_rows, block_rows, 0)
        return attend_block(query_rows, near_k, near_v, near_ok, far_k, far_v, far_bias, far_ok)

    results = lax.map(one_block, jnp.arange(block_count, dtype=jnp.int32))
    return results.reshape(frame_tokens, head_count, head_size)


def local(queries, key_tokens, values, near_list, near_count, dist_band, band_factor):
    tokens_dev = queries.shape[1]
    features = queries.shape[2]
    head_count = features // HD
    frame_index = lax.axis_index("tm")
    split_shape = (1, tokens_dev, head_count, HD)
    split_q, split_k, split_v = (
        lax.all_to_all(
            queries.reshape(split_shape), "space", split_axis=2, concat_axis=1, tiled=True
        ),
        lax.all_to_all(
            key_tokens.reshape(split_shape), "space", split_axis=2, concat_axis=1, tiled=True
        ),
        lax.all_to_all(
            values.reshape(split_shape), "space", split_axis=2, concat_axis=1, tiled=True
        ),
    )
    head_pair = jnp.stack([split_k, split_v], axis=1)
    rim_heads = extended(head_pair, (("tm", 0),), 1)
    key_rim = rim_heads[:, 0]
    value_rim = rim_heads[:, 1]
    frame_tokens = key_rim.shape[1]
    local_heads = key_rim.shape[2]
    own_pair = jnp.stack([key_rim[1], value_rim[1]], axis=0)
    pooled_heads = jnp.mean(
        own_pair.reshape(2, frame_tokens // POOL, POOL, local_heads, HD), axis=2, dtype=jnp.float32
    ).astype(jnp.bfloat16)
    far_pair = lax.all_gather(pooled_heads[None], "tm", axis=0, tiled=True)
    lists = lax.dynamic_index_in_dim(near_list, frame_index, 0, keepdims=False)
    counts = lax.dynamic_index_in_dim(near_count, frame_index, 0, keepdims=False)
    frame_output = attend_frame(
        split_q[0],
        key_rim,
        value_rim,
        far_pair[:, 0],
        far_pair[:, 1],
        lists,
        counts,
        dist_band,
        band_factor,
        frame_index,
    )
    returned = lax.all_to_all(frame_output[None], "space", split_axis=1, concat_axis=2, tiled=True)
    return returned.reshape(1, tokens_dev, features)


def solution(mesh):
    return jax.shard_map(
        local,
        mesh=mesh,
        in_specs=(
            P("tm", "space", None),
            P("tm", "space", None),
            P("tm", "space", None),
            P(),
            P(),
            P(),
            P(),
        ),
        out_specs=P("tm", "space", None),
        check_vma=False,
    )
```

profile of v0, /device:TPU:0, one launch (start us, length us, event | category | flops | bytes accessed | tf_op | source)
XLA Modules:
  0.0 123.3 jit_solution(3960450113721223402)
XLA Ops:
  0.0 1.8 %copy.51 = bf16[1,256,512]{1,2,0:T(8,128)(2,1)} copy(bf16[1,256,512]{2,1,0:T(8,128)(2,1)} %param.12) | data formatting | bytes 524288 | tf_op args[1]
  1.8 6.3 %all-to-all-start = ((bf16[1,256,4,128]{1,3,0,2:T(8,128)(2,1)}), bf16[1,256,4,128]{1,3,0,2:T(8,128)(2,1)S(1)}, u32[]{:S(2)}, u32[]{:S(2)}) async-start(bf16[1,256,4,128]{1,3,0,2:T(8,128)(2,1)} %bitcast.2), calls=%async_computation | async-start | bytes 524288 | tf_op jit(solution)/shard_map/all_to_all | solution.py:135
  10.1 1.8 %copy.54 = bf16[1,256,512]{1,2,0:T(8,128)(2,1)} copy(bf16[1,256,512]{2,1,0:T(8,128)(2,1)} %param.13) | data formatting | bytes 524288 | tf_op args[2]
  11.9 1.8 %copy.57 = bf16[1,256,512]{1,2,0:T(8,128)(2,1)} copy(bf16[1,256,512]{2,1,0:T(8,128)(2,1)} %param.11) | data formatting | bytes 524288 | tf_op args[0]
  13.8 3.2 %all-to-all-done = bf16[1,256,4,128]{1,3,0,2:T(8,128)(2,1)S(1)} async-done(((bf16[1,256,4,128]{1,3,0,2:T(8,128)(2,1)}), bf16[1,256,4,128]{1,3,0,2:T(8,128)(2,1)S(1)}, u32[]{:S(2)}, u32[]{:S(2)}) %all-to-all-start) | async-done | bytes 262176 | tf_op jit(solution)/shard_map/all_to_all | solution.py:135
  17.0 3.4 %all-to-all-start.1 = ((bf16[1,256,4,128]{1,3,0,2:T(8,128)(2,1)}), bf16[1,256,4,128]{1,3,0,2:T(8,128)(2,1)S(1)}, u32[]{:S(2)}, u32[]{:S(2)}) async-start(bf16[1,256,4,128]{1,3,0,2:T(8,128)(2,1)} %bitcast.7), calls=%async_computation.1 | async-start | bytes 524288 | tf_op jit(solution)/shard_map/all_to_all | solution.py:138
  20.7 6.8 %all-to-all-done.1 = bf16[1,256,4,128]{1,3,0,2:T(8,128)(2,1)S(1)} async-done(((bf16[1,256,4,128]{1,3,0,2:T(8,128)(2,1)}), bf16[1,256,4,128]{1,3,0,2:T(8,128)(2,1)S(1)}, u32[]{:S(2)}, u32[]{:S(2)}) %all-to-all-start.1) | async-done | bytes 262176 | tf_op jit(solution)/shard_map/all_to_all | solution.py:138
  27.5 3.4 %all-to-all-start.2 = ((bf16[1,256,4,128]{1,3,0,2:T(8,128)(2,1)}), bf16[1,256,4,128]{1,3,0,2:T(8,128)(2,1)S(1)}, u32[]{:S(2)}, u32[]{:S(2)}) async-start(bf16[1,256,4,128]{1,3,0,2:T(8,128)(2,1)} %bitcast.13), calls=%async_computation.2 | async-start | bytes 524288 | tf_op jit(solution)/shard_map/all_to_all | solution.py:132
  31.1 1.3 %collective-permute-start = (bf16[1,2,1024,1,128]{4,2,3,1,0:T(8,128)(2,1)S(1)}, bf16[1,2,1024,1,128]{4,2,3,1,0:T(8,128)(2,1)S(1)}, u32[]{:S(2)}, u32[]{:S(2)}) collective-permute-start(bf16[1,2,1024,1,128]{4,2,3,1,0:T(8,128)(2,1)S(1)} %pad_maximum_fusion.1), channel_id=1, source_target_pairs={{0,4},{4,8},{8,12},{12,16},{16,20},{20,24},{24,28},{1,5},{5,9},{9,... | collective-permute-start | bytes 1572872 | tf_op jit(solution)/shard_map/ppermute | solution.py:20
  32.4 1.3 %collective-permute-start.1 = (bf16[1,2,1024,1,128]{4,2,3,1,0:T(8,128)(2,1)S(1)}, bf16[1,2,1024,1,128]{4,2,3,1,0:T(8,128)(2,1)S(1)}, u32[]{:S(2)}, u32[]{:S(2)}) collective-permute-start(bf16[1,2,1024,1,128]{4,2,3,1,0:T(8,128)(2,1)S(1)} %pad_maximum_fusion.1), channel_id=1, source_target_pairs={{4,0},{8,4},{12,8},{16,12},{20,16},{24,20},{28,24},{5,1},{9,5},{13... | collective-permute-start | bytes 1572872 | tf_op jit(solution)/shard_map/ppermute | solution.py:23
  33.8 15.5 %all-gather = bf16[16,8,128]{2,1,0:T(8,128)(2,1)S(1)} all-gather(bf16[2,8,128]{2,1,0:T(8,128)(2,1)S(1)} %multiply_convert_fusion.4), channel_id=2, replica_groups=mesh['tm'=8,'space'=4] {'tm'}, dimensions={0}, use_global_device_ids=true | all-gather | bytes 36864 | tf_op jit(solution)/shard_map/all_gather | solution.py:152
  50.8 1.0 fusion.36
  51.7 51.8 %while.11 = (s32[]{:T(128)}, bf16[4,256,1,128]{3,1,0,2:T(8,128)(2,1)}, s32[4]{0:T(128)S(1)}, s32[4,8]{1,0:T(4,128)S(1)}, bf16[12,256,1,128]{3,1,0,2:T(8,128)(2,1...) while((s32[]{:T(128)}, ...), condition=%wide.region_12.14_spmd.clone, body=%wide.region_7.13_spmd.clone.sunk | while | flops 282329664 | bytes 14615961 | solution.py:121
  54.3 1.8 %gather_fusion = bf16[8,256,128]{2,1,0:T(8,128)(2,1)S(1)} fusion(bf16[12,256,128]{2,1,0:T(8,128)(2,1)} %bitcast.129, s32[1024]{0:T(1024)S(1)} %pad_clamp_fusion.2), kind=kCustom, calls=%fused_computation.clone.clone.1 | custom fusion | bytes 1048608 | tf_op jit(solution)/shard_map/while/body/eval_jaxpr/jit(_take)/gather | solution.py:114
  56.8 1.0 bitcast_select_fusion.5
  59.8 1.4 %fusion.55 = (f32[256]{0:T(256)S(1)}, f32[256,2048]{1,0:T(8,128)S(1)}) fusion(bf16[2048,128]{1,0:T(8,128)(2,1)S(1)} %bitcast.134, bf16[1024,1,128]{2,0,1:T(8,128)(2,1)} %get-tuple-element.267, s32[]{:T(128)S(6)} %select_n.160, pred[2048]{0:T(1024)(128)(4,1)S(1)} %broadcast_in_dim.258), kind=kOutput, calls=%fused_computation.71.clone.1 | convolution fusion | flops 135790336 | bytes 2690052 | tf_op jit(solution)/shard_map/while/body/eval_jaxpr/bhd,khd->hbk/dot_general | solution.py:54
  61.5 1.0 fusion.54
  67.3 1.8 %gather_fusion = bf16[8,256,128]{2,1,0:T(8,128)(2,1)S(1)} fusion(bf16[12,256,128]{2,1,0:T(8,128)(2,1)} %bitcast.129, s32[1024]{0:T(1024)S(1)} %pad_clamp_fusion.2), kind=kCustom, calls=%fused_computation.clone.clone.1 | custom fusion | bytes 1048608 | tf_op jit(solution)/shard_map/while/body/eval_jaxpr/jit(_take)/gather | solution.py:114
  69.7 1.0 bitcast_select_fusion.5
  72.7 1.4 %fusion.55 = (f32[256]{0:T(256)S(1)}, f32[256,2048]{1,0:T(8,128)S(1)}) fusion(bf16[2048,128]{1,0:T(8,128)(2,1)S(1)} %bitcast.134, bf16[1024,1,128]{2,0,1:T(8,128)(2,1)} %get-tuple-element.267, s32[]{:T(128)S(6)} %select_n.160, pred[2048]{0:T(1024)(128)(4,1)S(1)} %broadcast_in_dim.258), kind=kOutput, calls=%fused_computation.71.clone.1 | convolution fusion | flops 135790336 | bytes 2690052 | tf_op jit(solution)/shard_map/while/body/eval_jaxpr/bhd,khd->hbk/dot_general | solution.py:54
  74.4 1.0 fusion.54
  80.3 1.8 %gather_fusion = bf16[8,256,128]{2,1,0:T(8,128)(2,1)S(1)} fusion(bf16[12,256,128]{2,1,0:T(8,128)(2,1)} %bitcast.129, s32[1024]{0:T(1024)S(1)} %pad_clamp_fusion.2), kind=kCustom, calls=%fused_computation.clone.clone.1 | custom fusion | bytes 1048608 | tf_op jit(solution)/shard_map/while/body/eval_jaxpr/jit(_take)/gather | solution.py:114
  82.7 1.0 bitcast_select_fusion.5
  85.7 1.4 %fusion.55 = (f32[256]{0:T(256)S(1)}, f32[256,2048]{1,0:T(8,128)S(1)}) fusion(bf16[2048,128]{1,0:T(8,128)(2,1)S(1)} %bitcast.134, bf16[1024,1,128]{2,0,1:T(8,128)(2,1)} %get-tuple-element.267, s32[]{:T(128)S(6)} %select_n.160, pred[2048]{0:T(1024)(128)(4,1)S(1)} %broadcast_in_dim.258), kind=kOutput, calls=%fused_computation.71.clone.1 | convolution fusion | flops 135790336 | bytes 2690052 | tf_op jit(solution)/shard_map/while/body/eval_jaxpr/bhd,khd->hbk/dot_general | solution.py:54
  87.4 1.0 fusion.54
  93.2 1.8 %gather_fusion = bf16[8,256,128]{2,1,0:T(8,128)(2,1)S(1)} fusion(bf16[12,256,128]{2,1,0:T(8,128)(2,1)} %bitcast.129, s32[1024]{0:T(1024)S(1)} %pad_clamp_fusion.2), kind=kCustom, calls=%fused_computation.clone.clone.1 | custom fusion | bytes 1048608 | tf_op jit(solution)/shard_map/while/body/eval_jaxpr/jit(_take)/gather | solution.py:114
  95.7 1.0 bitcast_select_fusion.5
  98.7 1.4 %fusion.55 = (f32[256]{0:T(256)S(1)}, f32[256,2048]{1,0:T(8,128)S(1)}) fusion(bf16[2048,128]{1,0:T(8,128)(2,1)S(1)} %bitcast.134, bf16[1024,1,128]{2,0,1:T(8,128)(2,1)} %get-tuple-element.267, s32[]{:T(128)S(6)} %select_n.160, pred[2048]{0:T(1024)(128)(4,1)S(1)} %broadcast_in_dim.258), kind=kOutput, calls=%fused_computation.71.clone.1 | convolution fusion | flops 135790336 | bytes 2690052 | tf_op jit(solution)/shard_map/while/body/eval_jaxpr/bhd,khd->hbk/dot_general | solution.py:54
  100.4 1.0 fusion.54
  103.6 1.4 %copy.69 = bf16[1,1024,1,128]{3,2,0,1:T(2,128)(2,1)S(1)} copy(bf16[1,1024,1,128]{3,1,2,0:T(8,128)(2,1)} %bitcast.155) | data formatting | bytes 524288 | tf_op jit(solution)/shard_map/broadcast_in_dim;reshape | solution.py:167
  105.4 2.2 %reduce.19 = bf16[1024,128]{1,0:T(8,128)(2,1)S(1)} reduce(bf16[1024,1,1,128]{3,2,1,0:T(2,128)(2,1)S(1)} %bitcast.145, bf16[]{:T(256)} %broadcast.251), dimensions={1,2}, to_apply=%bitcast.101.reduce_sub_computation | reduce | bytes 524290
  107.7 14.2 %all_to_all.60 = bf16[4,2,16384]{2,1,0:T(2,128)(2,1)S(1)} all-to-all(bf16[4,2,16384]{2,1,0:T(2,128)(2,1)S(1)} %reshape.508), channel_id=1, replica_groups=mesh['tm'=8,'space'=4] {'space'}, dimensions={0} | all-to-all | bytes 524288 | tf_op jit(solution)/shard_map/all_to_all | solution.py:167
  (137 shorter events, 26.6 us)
Async XLA Ops:
  0.0 20.5 %copy-start = (s32[8,4,8]{2,1,0:T(4,128)S(1)}, s32[8,4,8]{2,1,0:T(4,128)}, u32[]{:S(2)}) copy-start(s32[8,4,8]{2,1,0:T(4,128)} %param.14) | copy-start | bytes 3076
  0.0 13.6 %copy-start.2 = (s32[8,4]{0,1:T(4,128)S(1)}, s32[8,4]{0,1:T(4,128)}, u32[]{:S(2)}) copy-start(s32[8,4]{0,1:T(4,128)} %param.15) | copy-start | bytes 388
  1.8 15.2 %all-to-all-start = ((bf16[1,256,4,128]{1,3,0,2:T(8,128)(2,1)}), bf16[1,256,4,128]{1,3,0,2:T(8,128)(2,1)S(1)}, u32[]{:S(2)}, u32[]{:S(2)}) async-start(bf16[1,256,4,128]{1,3,0,2:T(8,128)(2,1)} %bitcast.2), calls=%async_computation | async-start | bytes 524288 | tf_op jit(solution)/shard_map/all_to_all | solution.py:135
  17.0 10.4 %all-to-all-start.1 = ((bf16[1,256,4,128]{1,3,0,2:T(8,128)(2,1)}), bf16[1,256,4,128]{1,3,0,2:T(8,128)(2,1)S(1)}, u32[]{:S(2)}, u32[]{:S(2)}) async-start(bf16[1,256,4,128]{1,3,0,2:T(8,128)(2,1)} %bitcast.7), calls=%async_computation.1 | async-start | bytes 524288 | tf_op jit(solution)/shard_map/all_to_all | solution.py:138
  27.5 22.1 %all-to-all-start.2 = ((bf16[1,256,4,128]{1,3,0,2:T(8,128)(2,1)}), bf16[1,256,4,128]{1,3,0,2:T(8,128)(2,1)S(1)}, u32[]{:S(2)}, u32[]{:S(2)}) async-start(bf16[1,256,4,128]{1,3,0,2:T(8,128)(2,1)} %bitcast.13), calls=%async_computation.2 | async-start | bytes 524288 | tf_op jit(solution)/shard_map/all_to_all | solution.py:132
  31.1 19.4 %collective-permute-start = (bf16[1,2,1024,1,128]{4,2,3,1,0:T(8,128)(2,1)S(1)}, bf16[1,2,1024,1,128]{4,2,3,1,0:T(8,128)(2,1)S(1)}, u32[]{:S(2)}, u32[]{:S(2)}) collective-permute-start(bf16[1,2,1024,1,128]{4,2,3,1,0:T(8,128)(2,1)S(1)} %pad_maximum_fusion.1), channel_id=1, source_target_pairs={{0,4},{4,8},{8,12},{12,16},{16,20},{20,24},{24,28},{1,5},{5,9},{9,... | collective-permute-start | bytes 1572872 | tf_op jit(solution)/shard_map/ppermute | solution.py:20
  32.4 18.1 %collective-permute-start.1 = (bf16[1,2,1024,1,128]{4,2,3,1,0:T(8,128)(2,1)S(1)}, bf16[1,2,1024,1,128]{4,2,3,1,0:T(8,128)(2,1)S(1)}, u32[]{:S(2)}, u32[]{:S(2)}) collective-permute-start(bf16[1,2,1024,1,128]{4,2,3,1,0:T(8,128)(2,1)S(1)} %pad_maximum_fusion.1), channel_id=1, source_target_pairs={{4,0},{8,4},{12,8},{16,12},{20,16},{24,20},{28,24},{5,1},{9,5},{13... | collective-permute-start | bytes 1572872 | tf_op jit(solution)/shard_map/ppermute | solution.py:23
  61.2 2.2 %copy-start.1 = (bf16[8,256,1,128]{3,1,0,2:T(8,128)(2,1)S(1)}, bf16[8,256,1,128]{3,1,0,2:T(8,128)(2,1)}, u32[]{:S(2)}) copy-start(bf16[8,256,1,128]{3,1,0,2:T(8,128)(2,1)} %get-tuple-element.225) | copy-start | bytes 1572868 | tf_op jit(solution)/shard_map/while
  74.1 2.2 %copy-start.1 = (bf16[8,256,1,128]{3,1,0,2:T(8,128)(2,1)S(1)}, bf16[8,256,1,128]{3,1,0,2:T(8,128)(2,1)}, u32[]{:S(2)}) copy-start(bf16[8,256,1,128]{3,1,0,2:T(8,128)(2,1)} %get-tuple-element.225) | copy-start | bytes 1572868 | tf_op jit(solution)/shard_map/while
  87.1 2.2 %copy-start.1 = (bf16[8,256,1,128]{3,1,0,2:T(8,128)(2,1)S(1)}, bf16[8,256,1,128]{3,1,0,2:T(8,128)(2,1)}, u32[]{:S(2)}) copy-start(bf16[8,256,1,128]{3,1,0,2:T(8,128)(2,1)} %get-tuple-element.225) | copy-start | bytes 1572868 | tf_op jit(solution)/shard_map/while
  100.0 2.2 %copy-start.1 = (bf16[8,256,1,128]{3,1,0,2:T(8,128)(2,1)S(1)}, bf16[8,256,1,128]{3,1,0,2:T(8,128)(2,1)}, u32[]{:S(2)}) copy-start(bf16[8,256,1,128]{3,1,0,2:T(8,128)(2,1)} %get-tuple-element.225) | copy-start | bytes 1572868 | tf_op jit(solution)/shard_map/while
where the time goes:
time: 124 us; the launch traced here: 123 us
  local copies, waits for them, and re-layouts  30.9 us (25%)
  blocking collectives  29.7 us (24%)
  starting transfers between devices  15.7 us (13%)
  other arithmetic  13.3 us (11%)
  matrix products  12.8 us (10%)
  loops' own time  10.6 us (9%)
  waiting for transfers between devices  9.98 us (8%)
    all_gather x1, blocking collectives, local(): far_pair = lax.all_gather(pooled_heads[None], 'tm', axis=0, tiled=True)  15.5 us
    all_to_all x1, blocking collectives, local(): lax.all_to_all(frame_output[None], 'space', split_axis=1, concat_axis=2,...  14.2 us
    another operation x1, loops' own time, attend_frame(): results = lax.map(one_block, jnp.arange(block_count, dtype=jnp.int32))  10.6 us
    gather x4, local copies, waits for them, and re-layouts, one_block(): jnp.take(value_blocks, block_ids, axis=0)  7.12 us
    all_to_all x1, waiting for transfers between devices, local(): lax.all_to_all(values.reshape(split_shape), 'space', split_axis=2, concat...  6.76 us
    all_to_all x1, starting transfers between devices, local(): lax.all_to_all(key_tokens.reshape(split_shape), 'space', split_axis=2, co...  6.32 us
    unnamed x11, local copies, waits for them, and re-layouts  6.28 us
    dot_general x4, matrix products, attend_block(): jnp.einsum('bhd,khd->hbk', query_rows, near_k, preferred_element_type=jnp...  5.48 us
  transfers between devices with their start and end apart: 5, of which 2 were waited for; matrix products, arithmetic and copies ran while one was open for 6% of the time, Pallas kernels for 0%

commit v1 on v0

v1 whole, which is shorter than its diff:
```python
import functools
import math

import jax
import jax.numpy as jnp
from jax import lax
from jax.experimental import pallas as pl
from jax.experimental.pallas import tpu as pltpu
from jax.sharding import PartitionSpec as P

HD = 128
POOL = 128
LOWEST = -1e30
MESH = pl.DeviceIdType.MESH


def kernel(
    frames,
    parts,
    list_ref,
    count_ref,
    band_ref,
    factor_ref,
    q_ref,
    k_ref,
    v_ref,
    out_ref,
    q_buf,
    k_buf,
    v_buf,
    far_buf,
    far_k,
    far_v,
    far_bias,
    scores,
    staged,
    local_sem,
    swap_send,
    swap_recv,
    side_send,
    side_recv,
    pool_send,
    pool_recv,
    back_send,
    back_recv,
):
    frame = lax.axis_index("tm")
    part = lax.axis_index("space")
    rows = q_buf.shape[1]
    slots = list_ref.shape[2]
    far_rows = far_buf.shape[2]
    far_total = frames * far_rows

    def shifted(step):
        return lax.rem(part + step, parts)

    def columns(index):
        return pl.ds(pl.multiple_of(index * HD, HD), HD)

    barrier = pltpu.get_barrier_semaphore()
    for step in range(1, parts):
        pl.semaphore_signal(
            barrier, inc=1, device_id=(frame, shifted(step)), device_id_type=MESH
        )
    for step in range(1, frames):
        pl.semaphore_signal(
            barrier,
            inc=1,
            device_id=(lax.rem(frame + step, frames), part),
            device_id_type=MESH,
        )
    pl.semaphore_wait(barrier, parts - 1 + frames - 1)

    sources = (k_ref, v_ref, q_ref)

    def landing(which, index):
        if which == 2:
            return q_buf.at[index]
        return (k_buf, v_buf)[which].at[parts + index]

    def swap(which, target, slot):
        return pltpu.make_async_remote_copy(
            src_ref=sources[which].at[:, columns(target)],
            dst_ref=landing(which, slot),
            send_sem=swap_send.at[which, target],
            recv_sem=swap_recv.at[which, slot],
            device_id=(frame, target),
            device_id_type=MESH,
        )

    def side(which, direction, index):
        there = index if direction == 0 else 2 * parts + index
        buf = (k_buf, v_buf)[which]
        target = frame + 1 if direction == 0 else frame - 1
        return pltpu.make_async_remote_copy(
            src_ref=buf.at[parts + index],
            dst_ref=buf.at[there],
            send_sem=side_send.at[direction, which, index],
            recv_sem=side_recv.at[direction, which, index],
            device_id=(target, part),
            device_id_type=MESH,
        )

    own = [
        pltpu.make_async_copy(
            sources[which].at[:, columns(part)], landing(which, part), local_sem.at[which]
        )
        for which in range(3)
    ]
    for copy in own:
        copy.start()
    for which in range(3):
        for step in range(1, parts):
            swap(which, shifted(step), part).start()

    def forward(which, index):
        @pl.when(frame < frames - 1)
        def _():
            side(which, 0, index).start()

        @pl.when(frame > 0)
        def _():
            side(which, 1, index).start()

    own[0].wait()
    forward(0, part)
    own[1].wait()
    forward(1, part)
    for which in range(2):
        for step in range(1, parts):
            source = shifted(step)
            swap(which, source, source).wait_recv()
            forward(which, source)

    tokens = parts * rows
    pool_row = lax.broadcasted_iota(jnp.int32, (far_rows, tokens), 0)
    pool_col = lax.broadcasted_iota(jnp.int32, (far_rows, tokens), 1)
    average = jnp.where(pool_row == pool_col // POOL, 1.0 / POOL, 0.0).astype(jnp.bfloat16)
    for which, buf in enumerate((k_buf, v_buf)):
        frame_rows = buf[parts : 2 * parts].reshape(tokens, HD)
        pooled = jnp.dot(average, frame_rows, preferred_element_type=jnp.float32)
        far_buf[frame, which] = pooled.astype(jnp.bfloat16).astype(jnp.float32)

    def share(target, slot):
        return pltpu.make_async_remote_copy(
            src_ref=far_buf.at[slot],
            dst_ref=far_buf.at[slot],
            send_sem=pool_send.at[target],
            recv_sem=pool_recv.at[slot],
            device_id=(target, part),
            device_id_type=MESH,
        )

    for step in range(1, frames):
        share(lax.rem(frame + step, frames), frame).start()

    own[2].wait()
    for step in range(1, parts):
        source = shifted(step)
        swap(2, source, source).wait_recv()
    for step in range(1, frames):
        source = lax.rem(frame + step, frames)
        share(source, source).wait_recv()

    mix_row = lax.broadcasted_iota(jnp.int32, (far_total, far_total), 0)
    mix_col = lax.broadcasted_iota(jnp.int32, (far_total, far_total), 1)
    lane_frame = lax.broadcasted_iota(jnp.int32, (8, far_total), 1) // far_rows
    row_frame = mix_row // far_rows
    factor_rows = jnp.ones((far_total, far_total), jnp.int32)
    bias = jnp.full((8, far_total), LOWEST, jnp.float32)
    for other in range(frames):
        distance = jnp.abs(frame - other)
        band = band_ref[distance]
        factor = jnp.int32(1)
        for entry in range(factor_ref.shape[0]):
            factor = jnp.where(band == entry + 1, factor_ref[entry], factor)
        offset = jnp.where(
            factor == 1,
            jnp.float32(0.0),
            jnp.where(factor == 2, jnp.float32(-math.log(2.0)), jnp.float32(-math.log(4.0))),
        )
        offset = jnp.where(distance >= 2, offset, jnp.float32(LOWEST))
        factor_rows = jnp.where(row_frame == other, factor, factor_rows)
        bias = jnp.where(lane_frame == other, offset, bias)
    mix = jnp.where(
        factor_rows == 1,
        jnp.where(mix_row == mix_col, 1.0, 0.0),
        jnp.where(
            factor_rows == 2,
            jnp.where(mix_row // 2 == mix_col // 2, 0.5, 0.0),
            jnp.where(mix_row // 4 == mix_col // 4, 0.25, 0.0),
        ),
    ).astype(jnp.bfloat16)
    far_bias[...] = bias
    for which, far in enumerate((far_k, far_v)):
        pooled = far_buf[:, which].reshape(far_total, HD).astype(jnp.bfloat16)
        far[...] = jnp.dot(mix, pooled, preferred_element_type=jnp.float32).astype(jnp.bfloat16)

    for which in range(2):
        for index in range(parts):

            @pl.when(frame > 0)
            def _(which=which, index=index):
                arrived = (k_buf, v_buf)[which].at[index]
                pltpu.make_async_remote_copy(
                    src_ref=arrived,
                    dst_ref=arrived,
                    send_sem=side_send.at[0, which, index],
                    recv_sem=side_recv.at[0, which, index],
                    device_id=(frame - 1, part),
                    device_id_type=MESH,
                ).wait_recv()

            @pl.when(frame < frames - 1)
            def _(which=which, index=index):
                arrived = (k_buf, v_buf)[which].at[2 * parts + index]
                pltpu.make_async_remote_copy(
                    src_ref=arrived,
                    dst_ref=arrived,
                    send_sem=side_send.at[1, which, index],
                    recv_sem=side_recv.at[1, which, index],
                    device_id=(frame + 1, part),
                    device_id_type=MESH,
                ).wait_recv()

    scale = 1.0 / math.sqrt(HD)
    contract = (((1,), (1,)), ((), ()))

    def attend(block):
        query = q_buf[block]
        live = count_ref[frame, block]
        near_wide = slots * rows
        far_scores = (
            lax.dot_general(query, far_k[...], contract, preferred_element_type=jnp.float32)
            * scale
            + far_bias[0:1, :]
        )
        top = jnp.max(far_scores, axis=1, keepdims=True)
        for slot in range(slots):
            keys = k_buf[list_ref[frame, block, slot]]
            hidden = jnp.where(slot < live, jnp.float32(0.0), jnp.float32(LOWEST))
            part_scores = (
                lax.dot_general(query, keys, contract, preferred_element_type=jnp.float32) * scale
                + hidden
            )
            scores[:, slot * rows : (slot + 1) * rows] = part_scores
            top = jnp.maximum(top, jnp.max(part_scores, axis=1, keepdims=True))
        weights = jnp.exp(far_scores - top)
        total = jnp.sum(weights, axis=1, keepdims=True)
        summed = jnp.dot(
            weights.astype(jnp.bfloat16), far_v[...], preferred_element_type=jnp.float32
        )
        for slot in range(slots):
            near_values = v_buf[list_ref[frame, block, slot]]
            weights = jnp.exp(scores[:, slot * rows : (slot + 1) * rows] - top)
            total = total + jnp.sum(weights, axis=1, keepdims=True)
            summed = summed + jnp.dot(
                weights.astype(jnp.bfloat16), near_values, preferred_element_type=jnp.float32
            )
        return (summed / total).astype(jnp.bfloat16)

    def back(target, slot):
        return pltpu.make_async_remote_copy(
            src_ref=staged.at[target],
            dst_ref=out_ref.at[:, columns(slot)],
            send_sem=back_send.at[target],
            recv_sem=back_recv.at[slot],
            device_id=(frame, target),
            device_id_type=MESH,
        )

    def one(step, carry):
        target = lax.rem(part + step, parts)
        staged[target] = attend(target)
        back(target, part).start()
        return carry

    lax.fori_loop(1, parts, one, 0)
    out_ref[:, columns(part)] = attend(part)

    for step in range(1, parts):
        other = shifted(step)
        back(other, other).wait_recv()
        back(other, part).wait_send()
        for which in range(3):
            swap(which, other, part).wait_send()
    for step in range(1, frames):
        share(lax.rem(frame + step, frames), frame).wait_send()
    for which in range(2):
        for index in range(parts):

            @pl.when(frame < frames - 1)
            def _(which=which, index=index):
                side(which, 0, index).wait_send()

            @pl.when(frame > 0)
            def _(which=which, index=index):
                side(which, 1, index).wait_send()


def local(frames, parts, queries, key_tokens, values, near_list, near_count, dist_band, band_factor):
    _, rows, features = queries.shape
    far_rows = parts * rows // POOL
    far_total = frames * far_rows
    slots = near_list.shape[2]
    smem = pl.BlockSpec(memory_space=pltpu.SMEM)
    anywhere = pl.BlockSpec(memory_space=pl.ANY)
    dma = pltpu.SemaphoreType.DMA
    out = pl.pallas_call(
        functools.partial(kernel, frames, parts),
        out_shape=jax.ShapeDtypeStruct((rows, features), jnp.bfloat16),
        in_specs=[smem] * 4 + [anywhere] * 3,
        out_specs=pl.BlockSpec(memory_space=pltpu.VMEM),
        scratch_shapes=[
            pltpu.VMEM((parts, rows, HD), jnp.bfloat16),
            pltpu.VMEM((3 * parts, rows, HD), jnp.bfloat16),
            pltpu.VMEM((3 * parts, rows, HD), jnp.bfloat16),
            pltpu.VMEM((frames, 2, far_rows, HD), jnp.float32),
            pltpu.VMEM((far_total, HD), jnp.bfloat16),
            pltpu.VMEM((far_total, HD), jnp.bfloat16),
            pltpu.VMEM((8, far_total), jnp.float32),
            pltpu.VMEM((rows, slots * rows), jnp.float32),
            pltpu.VMEM((parts, rows, HD), jnp.bfloat16),
            dma((3,)),
            dma((3, parts)),
            dma((3, parts)),
            dma((2, 2, parts)),
            dma((2, 2, parts)),
            dma((frames,)),
            dma((frames,)),
            dma((parts,)),
            dma((parts,)),
        ],
        compiler_params=pltpu.CompilerParams(
            collective_id=0, has_side_effects=True, vmem_limit_bytes=40 * 2**20
        ),
        cost_estimate=pl.CostEstimate(
            flops=4 * parts * rows * (slots * rows + far_total) * HD,
            bytes_accessed=8 * rows * features,
            transcendentals=parts * rows * (slots * rows + far_total),
        ),
    )(
        near_list,
        near_count,
        dist_band,
        band_factor,
        queries[0],
        key_tokens[0],
        values[0],
    )
    return out[None]


def solution(mesh):
    return jax.shard_map(
        functools.partial(local, mesh.shape["tm"], mesh.shape["space"]),
        mesh=mesh,
        in_specs=(
            P("tm", "space", None),
            P("tm", "space", None),
            P("tm", "space", None),
            P(),
            P(),
            P(),
            P(),
        ),
        out_specs=P("tm", "space", None),
        check_vma=False,
    )
```

time: 124 us -> 41.8 us (0.34)
  Pallas kernels: 0 us -> 35.8 us
  blocking collectives: 29.7 us -> 0 us
  local copies, waits for them, and re-layouts: 30.9 us -> 5.62 us
  starting transfers between devices: 15.7 us -> 0 us
  other arithmetic: 13.3 us -> 0 us
  matrix products: 12.8 us -> 0 us
  loops' own time: 10.6 us -> 0 us
  waiting for transfers between devices: 9.98 us -> 0 us
    pallas_call x0 -> x1, Pallas kernels: none -> 35.8 us  [local(): pl.pallas_call(functools.partial(kernel, frames, parts), out_shape=jax.Sh...]
    all_gather x1 -> x0, blocking collectives: 15.5 us -> none  [local(): far_pair = lax.all_gather(pooled_heads[None], 'tm', axis=0, tiled=True)]
    all_to_all x1 -> x0, blocking collectives: 14.2 us -> none  [local(): lax.all_to_all(frame_output[None], 'space', split_axis=1, concat_axis=2,...]
    all_to_all x3 -> x0, starting transfers between devices: 13.1 us -> none  [the longest x1 6.32 us: local(): lax.all_to_all(key_tokens.reshape(split_shape), 'space', split_axis=2, co...]
    dot_general x16 -> x0, matrix products: 12.8 us -> none  [the longest x4 5.48 us: attend_block(): jnp.einsum('bhd,khd->hbk', query_rows, near_k, preferred_element_type=jnp...]
    another operation x1 -> x0, loops' own time: 10.6 us -> none  [attend_frame(): results = lax.map(one_block, jnp.arange(block_count, dtype=jnp.int32))]
    all_to_all x3 -> x0, waiting for transfers between devices: 9.97 us -> none  [the longest x1 6.76 us: local(): lax.all_to_all(values.reshape(split_shape), 'space', split_axis=2, concat...]
    gather x8 -> x0, local copies, waits for them, and re-layouts: 9.71 us -> none  [the longest x4 7.12 us: one_block(): jnp.take(value_blocks, block_ids, axis=0)]
  transfers between devices with their start and end apart: 5 -> 0, of which waited for: 2 -> 0; matrix products, arithmetic and copies ran while one was open for 6% -> 0% of each run, Pallas kernels for 0% -> 0%
where the time goes in v1:
time: 41.8 us; the launch traced here: 41.5 us
  Pallas kernels  35.8 us (86%)
  local copies, waits for them, and re-layouts  5.62 us (13%)
    pallas_call x1, Pallas kernels, local(): pl.pallas_call(functools.partial(kernel, frames, parts), out_shape=jax.Sh...  35.8 us
    unnamed x16, local copies, waits for them, and re-layouts  5.62 us

profile of v1, /device:TPU:0, one launch (start us, length us, event | category | flops | bytes accessed | tf_op | source)
XLA Modules:
  0.0 41.5 jit_solution(10834511696658304407)
XLA Ops:
  0.0 0.0 copy-start.6
  0.0 0.7 %copy-done.6 = s32[8,4]{0,1:T(4,128)S(1)} copy-done((s32[8,4]{0,1:T(4,128)S(1)}, s32[8,4]{0,1:T(4,128)}, u32[]{:S(2)}) %copy-start.6) | copy-done | bytes 152
  0.7 0.0 copy-start.4
  0.7 0.0 copy-start.5
  0.7 0.1 copy.8.count_ref
  0.8 0.6 %copy-done.4 = s32[8]{0:T(128)S(1)} copy-done((s32[8]{0:T(128)S(1)}, s32[8]{0:T(128)}, u32[]{:S(2)}) %copy-start.4) | copy-done | bytes 56
  1.3 0.0 copy-done.5
  1.4 0.0 copy-start
  1.4 0.9 %copy-done = bf16[1,256,512]{2,1,0:T(8,128)(2,1)S(1)} copy-done((bf16[1,256,512]{2,1,0:T(8,128)(2,1)S(1)}, bf16[1,256,512]{2,1,0:T(8,128)(2,1)}, u32[]{:S(2)}) %copy-start) | copy-done | bytes 262168
  2.3 0.0 copy-start.1
  2.3 0.9 %copy-done.1 = bf16[1,256,512]{2,1,0:T(8,128)(2,1)S(1)} copy-done((bf16[1,256,512]{2,1,0:T(8,128)(2,1)S(1)}, bf16[1,256,512]{2,1,0:T(8,128)(2,1)}, u32[]{:S(2)}) %copy-start.1) | copy-done | bytes 262168
  3.3 0.0 copy-start.2
  3.3 0.9 %copy-done.2 = bf16[1,256,512]{2,1,0:T(8,128)(2,1)S(1)} copy-done((bf16[1,256,512]{2,1,0:T(8,128)(2,1)S(1)}, bf16[1,256,512]{2,1,0:T(8,128)(2,1)}, u32[]{:S(2)}) %copy-start.2) | copy-done | bytes 262168
  4.2 0.0 copy-start.3
  4.2 0.7 %copy-done.3 = s32[8,4,8]{2,1,0:T(4,128)S(1)} copy-done((s32[8,4,8]{2,1,0:T(4,128)S(1)}, s32[8,4,8]{2,1,0:T(4,128)}, u32[]{:S(2)}) %copy-start.3) | copy-done | bytes 1048
  4.9 35.8 %shard_map.73 = bf16[256,512]{1,0:T(8,128)(2,1)S(1)} custom-call(s32[8,4,8]{2,1,0:T(4,128)S(1)} %copy-done.3, s32[8,4]{1,0:T(8,128)S(1)} %copy.8.count_ref, s32[8]{0:T(128)S(1)} %copy-done.4, s32[3]{0:T(128)S(1)} %copy-done.5, bf16[256,512]{1,0:T(8,128)(2,1)S(1)} %bitcast.5, bf16[256,512]{1,0:T(8,128)(2,1)S(1)} %bitcast.6, bf16[256,512]{1,0:T(8,128)(2,1)S(1)} %bitcast.7), custom_call_target="tpu_custom_call" | custom-call | flops 1107296256 | bytes 1048576 | tf_op jit(solution)/shard_map/pallas_call | solution.py:309
  40.8 0.7 %copy.10 = bf16[1,256,512]{2,1,0:T(8,128)(2,1)} copy(bf16[1,256,512]{2,1,0:T(8,128)(2,1)S(1)} %bitcast.4) | data formatting | bytes 524288
Async XLA Ops:
  0.0 0.7 %copy-start.6 = (s32[8,4]{0,1:T(4,128)S(1)}, s32[8,4]{0,1:T(4,128)}, u32[]{:S(2)}) copy-start(s32[8,4]{0,1:T(4,128)} %param.11) | copy-start | bytes 388
  0.7 0.7 %copy-start.4 = (s32[8]{0:T(128)S(1)}, s32[8]{0:T(128)}, u32[]{:S(2)}) copy-start(s32[8]{0:T(128)} %band_ref.1) | copy-start | bytes 100
  0.7 0.7 %copy-start.5 = (s32[3]{0:T(128)S(1)}, s32[3]{0:T(128)}, u32[]{:S(2)}) copy-start(s32[3]{0:T(128)} %factor_ref.1) | copy-start | bytes 40
  1.4 0.9 %copy-start = (bf16[1,256,512]{2,1,0:T(8,128)(2,1)S(1)}, bf16[1,256,512]{2,1,0:T(8,128)(2,1)}, u32[]{:S(2)}) copy-start(bf16[1,256,512]{2,1,0:T(8,128)(2,1)} %param.7) | copy-start | bytes 786436
  2.3 0.9 %copy-start.1 = (bf16[1,256,512]{2,1,0:T(8,128)(2,1)S(1)}, bf16[1,256,512]{2,1,0:T(8,128)(2,1)}, u32[]{:S(2)}) copy-start(bf16[1,256,512]{2,1,0:T(8,128)(2,1)} %param.8) | copy-start | bytes 786436
  3.3 0.9 %copy-start.2 = (bf16[1,256,512]{2,1,0:T(8,128)(2,1)S(1)}, bf16[1,256,512]{2,1,0:T(8,128)(2,1)}, u32[]{:S(2)}) copy-start(bf16[1,256,512]{2,1,0:T(8,128)(2,1)} %param.9) | copy-start | bytes 786436
  4.2 0.7 %copy-start.3 = (s32[8,4,8]{2,1,0:T(4,128)S(1)}, s32[8,4,8]{2,1,0:T(4,128)}, u32[]{:S(2)}) copy-start(s32[8,4,8]{2,1,0:T(4,128)} %list_ref.1) | copy-start | bytes 3076

commit v2 on v1

v2 whole, which is shorter than its diff:
```python
import functools
import math

import jax
import jax.numpy as jnp
from jax import lax
from jax.experimental import pallas as pl
from jax.experimental.pallas import tpu as pltpu
from jax.sharding import PartitionSpec as P

HD = 128
POOL = 128
LOWEST = -1e30
MESH = pl.DeviceIdType.MESH


def kernel(
    frames,
    parts,
    list_ref,
    count_ref,
    band_ref,
    factor_ref,
    q_ref,
    k_ref,
    v_ref,
    out_ref,
    k_rows,
    v_rows,
    q_buf,
    k_buf,
    v_buf,
    pool_out,
    far_buf,
    far_k,
    far_v,
    far_bias,
    scores,
    near_weights,
    far_weights,
    totals,
    staged,
    local_sem,
    swap_send,
    swap_recv,
    side_send,
    side_recv,
    part_send,
    part_recv,
    pool_send,
    pool_recv,
    back_send,
    back_recv,
):
    frame = lax.axis_index("tm")
    part = lax.axis_index("space")
    rows = q_buf.shape[1]
    slots = list_ref.shape[2]
    each = rows // POOL
    far_rows = parts * each
    far_total = frames * far_rows
    steps = [(parts // 2 - 1 + i) % (parts - 1) + 1 for i in range(parts - 1)]

    def shifted(step):
        return lax.rem(part + step, parts)

    def columns(index):
        return pl.ds(pl.multiple_of(index * HD, HD), HD)

    sources = (k_ref, v_ref, q_ref)

    def landing(which, index):
        if which == 2:
            return q_buf.at[index]
        return (k_buf, v_buf)[which].at[parts + index]

    whole = [
        pltpu.make_async_copy(k_ref, k_rows, local_sem.at[3]),
        pltpu.make_async_copy(v_ref, v_rows, local_sem.at[4]),
    ]
    own = [
        pltpu.make_async_copy(
            sources[which].at[:, columns(part)], landing(which, part), local_sem.at[which]
        )
        for which in range(3)
    ]
    for copy in whole + own:
        copy.start()

    barrier = pltpu.get_barrier_semaphore()
    for step in range(1, parts):
        pl.semaphore_signal(
            barrier, inc=1, device_id=(frame, shifted(step)), device_id_type=MESH
        )
    for step in range(1, frames):
        pl.semaphore_signal(
            barrier,
            inc=1,
            device_id=(lax.rem(frame + step, frames), part),
            device_id_type=MESH,
        )
    pl.semaphore_wait(barrier, parts - 1 + frames - 1)

    def swap(which, target, slot):
        return pltpu.make_async_remote_copy(
            src_ref=sources[which].at[:, columns(target)],
            dst_ref=landing(which, slot),
            send_sem=swap_send.at[which, target],
            recv_sem=swap_recv.at[which, slot],
            device_id=(frame, target),
            device_id_type=MESH,
        )

    def side(which, direction, index):
        there = index if direction == 0 else 2 * parts + index
        buf = (k_buf, v_buf)[which]
        target = frame + 1 if direction == 0 else frame - 1
        return pltpu.make_async_remote_copy(
            src_ref=buf.at[parts + index],
            dst_ref=buf.at[there],
            send_sem=side_send.at[direction, which, index],
            recv_sem=side_recv.at[direction, which, index],
            device_id=(target, part),
            device_id_type=MESH,
        )

    def forward(which, index):
        @pl.when(frame < frames - 1)
        def _():
            side(which, 0, index).start()

        @pl.when(frame > 0)
        def _():
            side(which, 1, index).start()

    def arrivals(which):
        for index in range(parts):

            @pl.when(frame > 0)
            def _(index=index):
                arrived = (k_buf, v_buf)[which].at[index]
                pltpu.make_async_remote_copy(
                    src_ref=arrived,
                    dst_ref=arrived,
                    send_sem=side_send.at[0, which, index],
                    recv_sem=side_recv.at[0, which, index],
                    device_id=(frame - 1, part),
                    device_id_type=MESH,
                ).wait_recv()

            @pl.when(frame < frames - 1)
            def _(index=index):
                arrived = (k_buf, v_buf)[which].at[2 * parts + index]
                pltpu.make_async_remote_copy(
                    src_ref=arrived,
                    dst_ref=arrived,
                    send_sem=side_send.at[1, which, index],
                    recv_sem=side_recv.at[1, which, index],
                    device_id=(frame + 1, part),
                    device_id_type=MESH,
                ).wait_recv()

    def spread(target, slot):
        return pltpu.make_async_remote_copy(
            src_ref=pool_out.at[:, columns(target)],
            dst_ref=far_buf.at[frame, slot],
            send_sem=part_send.at[target],
            recv_sem=part_recv.at[slot],
            device_id=(frame, target),
            device_id_type=MESH,
        )

    def share(target, slot):
        return pltpu.make_async_remote_copy(
            src_ref=far_buf.at[slot],
            dst_ref=far_buf.at[slot],
            send_sem=pool_send.at[target],
            recv_sem=pool_recv.at[slot],
            device_id=(target, part),
            device_id_type=MESH,
        )

    for step in steps:
        swap(0, shifted(step), part).start()

    pool_row = lax.broadcasted_iota(jnp.int32, (8, rows), 0)
    pool_col = lax.broadcasted_iota(jnp.int32, (8, rows), 1) // POOL
    pooled = jnp.zeros((8, k_rows.shape[1]), jnp.float32)
    for which, taken in enumerate((k_rows, v_rows)):
        whole[which].wait()
        average = jnp.where(pool_row == pool_col + which * each, 1.0 / POOL, 0.0)
        pooled = pooled + jnp.dot(
            average.astype(jnp.bfloat16), taken[...], preferred_element_type=jnp.float32
        )
    pool_out[...] = pooled.astype(jnp.bfloat16).astype(jnp.float32)
    far_buf[frame, part] = pool_out[:, columns(part)]
    for step in steps:
        spread(shifted(step), part).start()

    for which in (2, 1):
        for step in steps:
            swap(which, shifted(step), part).start()

    for which in range(2):
        own[which].wait()
        forward(which, part)
    for step in steps:
        source = shifted(parts - step)
        swap(0, source, source).wait_recv()
        forward(0, source)
    for step in steps:
        source = shifted(parts - step)
        spread(source, source).wait_recv()
    for step in range(1, frames):
        share(lax.rem(frame + step, frames), frame).start()
    for step in range(1, frames):
        source = lax.rem(frame + step, frames)
        share(source, source).wait_recv()

    mix_row = lax.broadcasted_iota(jnp.int32, (far_rows, parts * 8), 0)
    mix_col = lax.broadcasted_iota(jnp.int32, (far_rows, parts * 8), 1)
    lane_frame = lax.broadcasted_iota(jnp.int32, (8, far_total), 1) // far_rows
    mixes = []
    for which in range(2):
        inner = mix_col % 8 - which * each
        held = (inner >= 0) & (inner < each)
        index = (mix_col // 8) * each + inner
        mixes.append(
            [
                jnp.where(held & (mix_row // e == index // e), 1.0 / e, 0.0)
                for e in (1, 2, 4)
            ]
        )
    bias = jnp.full((8, far_total), LOWEST, jnp.float32)
    for other in range(frames):
        distance = jnp.abs(frame - other)
        band = band_ref[distance]
        factor = jnp.int32(1)
        for entry in range(factor_ref.shape[0]):
            factor = jnp.where(band == entry + 1, factor_ref[entry], factor)
        offset = jnp.where(
            factor == 1,
            jnp.float32(0.0),
            jnp.where(factor == 2, jnp.float32(-math.log(2.0)), jnp.float32(-math.log(4.0))),
        )
        offset = jnp.where(distance >= 2, offset, jnp.float32(LOWEST))
        bias = jnp.where(lane_frame == other, offset, bias)
        pooled = far_buf[other].reshape(parts * 8, HD).astype(jnp.bfloat16)
        for which, far in enumerate((far_k, far_v)):
            once, pairs, quads = mixes[which]
            mix = jnp.where(factor == 1, once, jnp.where(factor == 2, pairs, quads))
            coarse = jnp.dot(
                mix.astype(jnp.bfloat16), pooled, preferred_element_type=jnp.float32
            )
            far[other] = coarse.astype(jnp.bfloat16).astype(jnp.float32)
    far_bias[...] = bias

    own[2].wait()
    for step in steps:
        source = shifted(parts - step)
        swap(2, source, source).wait_recv()
    arrivals(0)

    scale = 1.0 / math.sqrt(HD)
    contract = (((1,), (1,)), ((), ()))

    def weigh(block, carry):
        query = q_buf[block]
        live = count_ref[block, frame]
        far_scores = (
            lax.dot_general(
                query,
                far_k[...].reshape(far_total, HD).astype(jnp.bfloat16),
                contract,
                preferred_element_type=jnp.float32,
            )
            * scale
            + far_bias[0:1, :]
        )
        top = jnp.max(far_scores, axis=1, keepdims=True)
        for slot in range(slots):
            keys = k_buf[list_ref[frame, block, slot]]
            hidden = jnp.where(slot < live, jnp.float32(0.0), jnp.float32(LOWEST))
            near_scores = (
                lax.dot_general(query, keys, contract, preferred_element_type=jnp.float32) * scale
                + hidden
            )
            scores[:, slot * rows : (slot + 1) * rows] = near_scores
            top = jnp.maximum(top, jnp.max(near_scores, axis=1, keepdims=True))
        weights = jnp.exp(far_scores - top)
        total = jnp.sum(weights, axis=1, keepdims=True)
        far_weights[block] = weights.astype(jnp.bfloat16)
        for slot in range(slots):
            span = slice(slot * rows, (slot + 1) * rows)
            weights = jnp.exp(scores[:, span] - top)
            total = total + jnp.sum(weights, axis=1, keepdims=True)
            near_weights[block, :, span] = weights.astype(jnp.bfloat16)
        totals[block] = jnp.broadcast_to(total, (rows, HD))
        return carry

    lax.fori_loop(0, parts, weigh, 0)

    for step in steps:
        source = shifted(parts - step)
        swap(1, source, source).wait_recv()
        forward(1, source)
    arrivals(1)

    def attend(block):
        summed = jnp.dot(
            far_weights[block],
            far_v[...].reshape(far_total, HD).astype(jnp.bfloat16),
            preferred_element_type=jnp.float32,
        )
        for slot in range(slots):
            summed = summed + jnp.dot(
                near_weights[block, :, slot * rows : (slot + 1) * rows],
                v_buf[list_ref[frame, block, slot]],
                preferred_element_type=jnp.float32,
            )
        return (summed / totals[block]).astype(jnp.bfloat16)

    def back(target, slot):
        return pltpu.make_async_remote_copy(
            src_ref=staged.at[target],
            dst_ref=out_ref.at[:, columns(slot)],
            send_sem=back_send.at[target],
            recv_sem=back_recv.at[slot],
            device_id=(frame, target),
            device_id_type=MESH,
        )

    def one(i, carry):
        target = shifted((parts // 2 - 1 + i) % (parts - 1) + 1)
        staged[target] = attend(target)
        back(target, part).start()
        return carry

    lax.fori_loop(0, parts - 1, one, 0)
    out_ref[:, columns(part)] = attend(part)

    for step in steps:
        other = shifted(step)
        back(other, other).wait_recv()
        back(other, part).wait_send()
        spread(other, part).wait_send()
        for which in range(3):
            swap(which, other, part).wait_send()
    for step in range(1, frames):
        share(lax.rem(frame + step, frames), frame).wait_send()
    for which in range(2):
        for index in range(parts):

            @pl.when(frame < frames - 1)
            def _(which=which, index=index):
                side(which, 0, index).wait_send()

            @pl.when(frame > 0)
            def _(which=which, index=index):
                side(which, 1, index).wait_send()


def local(frames, parts, queries, key_tokens, values, near_list, near_count, dist_band, band_factor):
    _, rows, features = queries.shape
    far_rows = parts * rows // POOL
    far_total = frames * far_rows
    slots = near_list.shape[2]
    smem = pl.BlockSpec(memory_space=pltpu.SMEM)
    anywhere = pl.BlockSpec(memory_space=pl.ANY)
    dma = pltpu.SemaphoreType.DMA
    out = pl.pallas_call(
        functools.partial(kernel, frames, parts),
        out_shape=jax.ShapeDtypeStruct((rows, features), jnp.bfloat16),
        in_specs=[smem] * 4 + [anywhere] * 3,
        out_specs=pl.BlockSpec(memory_space=pltpu.VMEM),
        scratch_shapes=[
            pltpu.VMEM((rows, features), jnp.bfloat16),
            pltpu.VMEM((rows, features), jnp.bfloat16),
            pltpu.VMEM((parts, rows, HD), jnp.bfloat16),
            pltpu.VMEM((3 * parts, rows, HD), jnp.bfloat16),
            pltpu.VMEM((3 * parts, rows, HD), jnp.bfloat16),
            pltpu.VMEM((8, features), jnp.float32),
            pltpu.VMEM((frames, parts, 8, HD), jnp.float32),
            pltpu.VMEM((frames, far_rows, HD), jnp.float32),
            pltpu.VMEM((frames, far_rows, HD), jnp.float32),
            pltpu.VMEM((8, far_total), jnp.float32),
            pltpu.VMEM((rows, slots * rows), jnp.float32),
            pltpu.VMEM((parts, rows, slots * rows), jnp.bfloat16),
            pltpu.VMEM((parts, rows, far_total), jnp.bfloat16),
            pltpu.VMEM((parts, rows, HD), jnp.float32),
            pltpu.VMEM((parts, rows, HD), jnp.bfloat16),
            dma((5,)),
            dma((3, parts)),
            dma((3, parts)),
            dma((2, 2, parts)),
            dma((2, 2, parts)),
            dma((parts,)),
            dma((parts,)),
            dma((frames,)),
            dma((frames,)),
            dma((parts,)),
            dma((parts,)),
        ],
        compiler_params=pltpu.CompilerParams(
            collective_id=0, has_side_effects=True, vmem_limit_bytes=62 * 2**20
        ),
        cost_estimate=pl.CostEstimate(
            flops=4 * parts * rows * (slots * rows + far_total) * HD,
            bytes_accessed=8 * rows * features,
            transcendentals=parts * rows * (slots * rows + far_total),
        ),
    )(
        near_list,
        near_count.T,
        dist_band,
        band_factor,
        queries[0],
        key_tokens[0],
        values[0],
    )
    return out[None]


def solution(mesh):
    return jax.shard_map(
        functools.partial(local, mesh.shape["tm"], mesh.shape["space"]),
        mesh=mesh,
        in_specs=(
            P("tm", "space", None),
            P("tm", "space", None),
            P("tm", "space", None),
            P(),
            P(),
            P(),
            P(),
        ),
        out_specs=P("tm", "space", None),
        check_vma=False,
    )
```

time: 41.8 us -> 41.2 us (0.986)
  the two profiles are of different devices: /device:TPU:0 before, /device:TPU:1 now
where the time goes in v2:
time: 41.2 us; the launch traced here: 41 us
  Pallas kernels  39.4 us (96%)
  local copies, waits for them, and re-layouts  1.67 us (4%)
    pallas_call x1, Pallas kernels, local(): pl.pallas_call(functools.partial(kernel, frames, parts), out_shape=jax.Sh...  39.4 us
    unnamed x1, local copies, waits for them, and re-layouts  1.67 us

profile of v2, /device:TPU:1, one launch (start us, length us, event | category | flops | bytes accessed | tf_op | source)
XLA Modules:
  0.0 41.0 jit_solution(17532022800776623262)
XLA Ops:
  0.0 39.4 %shard_map.73 = bf16[256,512]{1,0:T(8,128)(2,1)} custom-call(s32[8,4,8]{2,1,0:T(4,128)} %list_ref.1, s32[4,8]{1,0:T(4,128)} %bitcast.9, s32[8]{0:T(128)} %band_ref.1, s32[3]{0:T(128)} %factor_ref.1, bf16[256,512]{1,0:T(8,128)(2,1)} %bitcast.6, bf16[256,512]{1,0:T(8,128)(2,1)} %bitcast.7, bf16[256,512]{1,0:T(8,128)(2,1)} %bitcast.8), custom_call_target="tpu_custom_call" | custom-call | flops 1107296256 | bytes 1048576 | tf_op jit(solution)/shard_map/pallas_call | solution.py:371
  39.4 1.7 %copy.9 = bf16[1,256,512]{2,1,0:T(8,128)(2,1)} copy(bf16[1,256,512]{2,1,0:T(8,128)(2,1)} %bitcast.5) | data formatting | bytes 524288

commit v3 on v2

--- a/solution.py
+++ b/solution.py
@@ -25,8 +25,7 @@
     k_ref,
     v_ref,
     out_ref,
-    k_rows,
-    v_rows,
+    heads,
     q_buf,
     k_buf,
     v_buf,
@@ -40,7 +39,9 @@
     far_weights,
     totals,
     staged,
+    returned,
     local_sem,
+    head_sem,
     swap_send,
     swap_recv,
     side_send,
@@ -74,9 +75,16 @@
             return q_buf.at[index]
         return (k_buf, v_buf)[which].at[parts + index]
 
-    whole = [
-        pltpu.make_async_copy(k_ref, k_rows, local_sem.at[3]),
-        pltpu.make_async_copy(v_ref, v_rows, local_sem.at[4]),
+    split = [
+        [
+            pltpu.make_async_copy(
+                sources[which].at[:, head * HD : (head + 1) * HD],
+                heads.at[which, head],
+                head_sem.at[which, head],
+            )
+            for head in range(parts)
+        ]
+        for which in range(3)
     ]
     own = [
         pltpu.make_async_copy(
@@ -84,8 +92,9 @@
         )
         for which in range(3)
     ]
-    for copy in whole + own:
-        copy.start()
+    for which in (0, 2, 1):
+        for copy in split[which] + [own[which]]:
+            copy.start()
 
     barrier = pltpu.get_barrier_semaphore()
     for step in range(1, parts):
@@ -103,7 +112,7 @@
 
     def swap(which, target, slot):
         return pltpu.make_async_remote_copy(
-            src_ref=sources[which].at[:, columns(target)],
+            src_ref=heads.at[which, target],
             dst_ref=landing(which, slot),
             send_sem=swap_send.at[which, target],
             recv_sem=swap_recv.at[which, slot],
@@ -162,7 +171,7 @@
 
     def spread(target, slot):
         return pltpu.make_async_remote_copy(
-            src_ref=pool_out.at[:, columns(target)],
+            src_ref=pool_out.at[target],
             dst_ref=far_buf.at[frame, slot],
             send_sem=part_send.at[target],
             recv_sem=part_recv.at[slot],
@@ -180,24 +189,31 @@
             device_id_type=MESH,
         )
 
+    for copy in split[0]:
+        copy.wait()
     for step in steps:
         swap(0, shifted(step), part).start()
+    for which in (2, 1):
+        for copy in split[which]:
+            copy.wait()
 
     pool_row = lax.broadcasted_iota(jnp.int32, (8, rows), 0)
     pool_col = lax.broadcasted_iota(jnp.int32, (8, rows), 1) // POOL
-    pooled = jnp.zeros((8, k_rows.shape[1]), jnp.float32)
-    for which, taken in enumerate((k_rows, v_rows)):
-        whole[which].wait()
-        average = jnp.where(pool_row == pool_col + which * each, 1.0 / POOL, 0.0)
-        pooled = pooled + jnp.dot(
-            average.astype(jnp.bfloat16), taken[...], preferred_element_type=jnp.float32
-        )
-    pool_out[...] = pooled.astype(jnp.bfloat16).astype(jnp.float32)
-    far_buf[frame, part] = pool_out[:, columns(part)]
+    averages = [
+        jnp.where(pool_row == pool_col + which * each, 1.0 / POOL, 0.0).astype(jnp.bfloat16)
+        for which in range(2)
+    ]
+    for head in range(parts):
+        pooled = sum(
+            jnp.dot(averages[which], heads[which, head], preferred_element_type=jnp.float32)
+            for which in range(2)
+        )
+        pool_out[head] = pooled.astype(jnp.bfloat16).astype(jnp.float32)
+    far_buf[frame, part] = pool_out[part]
     for step in steps:
         spread(shifted(step), part).start()
 
-    for which in (2, 1):
+    for which in (1, 2):
         for step in steps:
             swap(which, shifted(step), part).start()
 
@@ -213,6 +229,10 @@
         spread(source, source).wait_recv()
     for step in range(1, frames):
         share(lax.rem(frame + step, frames), frame).start()
+    for step in steps:
+        source = shifted(parts - step)
+        swap(1, source, source).wait_recv()
+        forward(1, source)
     for step in range(1, frames):
         source = lax.rem(frame + step, frames)
         share(source, source).wait_recv()
@@ -300,10 +320,6 @@
 
     lax.fori_loop(0, parts, weigh, 0)
 
-    for step in steps:
-        source = shifted(parts - step)
-        swap(1, source, source).wait_recv()
-        forward(1, source)
     arrivals(1)
 
     def attend(block):
@@ -323,7 +339,7 @@
     def back(target, slot):
         return pltpu.make_async_remote_copy(
             src_ref=staged.at[target],
-            dst_ref=out_ref.at[:, columns(slot)],
+            dst_ref=returned.at[slot],
             send_sem=back_send.at[target],
             recv_sem=back_recv.at[slot],
             device_id=(frame, target),
@@ -337,11 +353,15 @@
         return carry
 
     lax.fori_loop(0, parts - 1, one, 0)
-    out_ref[:, columns(part)] = attend(part)
+    returned[part] = attend(part)
 
     for step in steps:
         other = shifted(step)
         back(other, other).wait_recv()
+    for head in range(parts):
+        out_ref[:, head * HD : (head + 1) * HD] = returned[head]
+    for step in steps:
+        other = shifted(step)
         back(other, part).wait_send()
         spread(other, part).wait_send()
         for which in range(3):
@@ -374,12 +394,11 @@
         in_specs=[smem] * 4 + [anywhere] * 3,
         out_specs=pl.BlockSpec(memory_space=pltpu.VMEM),
         scratch_shapes=[
-            pltpu.VMEM((rows, features), jnp.bfloat16),
-            pltpu.VMEM((rows, features), jnp.bfloat16),
+            pltpu.VMEM((3, parts, rows, HD), jnp.bfloat16),
             pltpu.VMEM((parts, rows, HD), jnp.bfloat16),
             pltpu.VMEM((3 * parts, rows, HD), jnp.bfloat16),
             pltpu.VMEM((3 * parts, rows, HD), jnp.bfloat16),
-            pltpu.VMEM((8, features), jnp.float32),
+            pltpu.VMEM((parts, 8, HD), jnp.float32),
             pltpu.VMEM((frames, parts, 8, HD), jnp.float32),
             pltpu.VMEM((frames, far_rows, HD), jnp.float32),
             pltpu.VMEM((frames, far_rows, HD), jnp.float32),
@@ -389,7 +408,9 @@
             pltpu.VMEM((parts, rows, far_total), jnp.bfloat16),
             pltpu.VMEM((parts, rows, HD), jnp.float32),
             pltpu.VMEM((parts, rows, HD), jnp.bfloat16),
-            dma((5,)),
+            pltpu.VMEM((parts, rows, HD), jnp.bfloat16),
+            dma((3,)),
+            dma((3, parts)),
             dma((3, parts)),
             dma((3, parts)),
             dma((2, 2, parts)),

time: 41.2 us -> 38.9 us (0.944)
  the two profiles are of different devices: /device:TPU:1 before, /device:TPU:0 now
where the time goes in v3:
time: 38.9 us; the launch traced here: 38.6 us
  Pallas kernels  36.9 us (95%)
  local copies, waits for them, and re-layouts  1.67 us (4%)
    pallas_call x1, Pallas kernels, local(): pl.pallas_call(functools.partial(kernel, frames, parts), out_shape=jax.Sh...  36.9 us
    unnamed x1, local copies, waits for them, and re-layouts  1.67 us

profile of v3, /device:TPU:0, one launch (start us, length us, event | category | flops | bytes accessed | tf_op | source)
XLA Modules:
  0.0 38.6 jit_solution(6156054906288161746)
XLA Ops:
  0.0 36.9 %shard_map.73 = bf16[256,512]{1,0:T(8,128)(2,1)} custom-call(s32[8,4,8]{2,1,0:T(4,128)} %list_ref.1, s32[4,8]{1,0:T(4,128)} %bitcast.9, s32[8]{0:T(128)} %band_ref.1, s32[3]{0:T(128)} %factor_ref.1, bf16[256,512]{1,0:T(8,128)(2,1)} %bitcast.6, bf16[256,512]{1,0:T(8,128)(2,1)} %bitcast.7, bf16[256,512]{1,0:T(8,128)(2,1)} %bitcast.8), custom_call_target="tpu_custom_call" | custom-call | flops 1107296256 | bytes 1048576 | tf_op jit(solution)/shard_map/pallas_call | solution.py:391
  37.0 1.7 %copy.9 = bf16[1,256,512]{2,1,0:T(8,128)(2,1)} copy(bf16[1,256,512]{2,1,0:T(8,128)(2,1)} %bitcast.5) | data formatting | bytes 524288

commit v4 on v3

--- a/solution.py
+++ b/solution.py
@@ -318,7 +318,6 @@
         totals[block] = jnp.broadcast_to(total, (rows, HD))
         return carry
 
-    lax.fori_loop(0, parts, weigh, 0)
 
     arrivals(1)
 
@@ -348,11 +347,13 @@
 
     def one(i, carry):
         target = shifted((parts // 2 - 1 + i) % (parts - 1) + 1)
+        weigh(target, 0)
         staged[target] = attend(target)
         back(target, part).start()
         return carry
 
     lax.fori_loop(0, parts - 1, one, 0)
+    weigh(part, 0)
     returned[part] = attend(part)
 
     for step in steps:

time: 38.9 us -> 37.3 us (0.959)
  Pallas kernels: 36.9 us -> 35.4 us
    pallas_call x1, Pallas kernels: 36.9 us -> 35.4 us  [local(): pl.pallas_call(functools.partial(kernel, frames, parts), out_shape=jax.Sh...]
where the time goes in v4:
time: 37.3 us; the launch traced here: 37 us
  Pallas kernels  35.4 us (95%)
  local copies, waits for them, and re-layouts  1.67 us (4%)
    pallas_call x1, Pallas kernels, local(): pl.pallas_call(functools.partial(kernel, frames, parts), out_shape=jax.Sh...  35.4 us
    unnamed x1, local copies, waits for them, and re-layouts  1.67 us

profile of v4, /device:TPU:0, one launch (start us, length us, event | category | flops | bytes accessed | tf_op | source)
XLA Modules:
  0.0 37.0 jit_solution(1953481313848754865)
XLA Ops:
  0.0 35.4 %shard_map.73 = bf16[256,512]{1,0:T(8,128)(2,1)} custom-call(s32[8,4,8]{2,1,0:T(4,128)} %list_ref.1, s32[4,8]{1,0:T(4,128)} %bitcast.9, s32[8]{0:T(128)} %band_ref.1, s32[3]{0:T(128)} %factor_ref.1, bf16[256,512]{1,0:T(8,128)(2,1)} %bitcast.6, bf16[256,512]{1,0:T(8,128)(2,1)} %bitcast.7, bf16[256,512]{1,0:T(8,128)(2,1)} %bitcast.8), custom_call_target="tpu_custom_call" | custom-call | flops 1107296256 | bytes 1048576 | tf_op jit(solution)/shard_map/pallas_call | solution.py:392
  35.4 1.7 %copy.9 = bf16[1,256,512]{2,1,0:T(8,128)(2,1)} copy(bf16[1,256,512]{2,1,0:T(8,128)(2,1)} %bitcast.5) | data formatting | bytes 524288
